TPU v7x, 32 devices: a whole 2x2x4 slice. The times are simulated.
32 devices in a mesh: nodes: 16 (over z, y, x), feat: 2 (over core).
Axes of the slice: x: 2, y: 2, z: 4, core: 2. Of those that a mesh axis runs over, the one named last changes fastest.
Arguments:
- grid_in: bfloat16 [4, 8192, 227], P(None, ('nodes', 'feat')), may hold values from -6 to 6
- targets: bfloat16 [4, 8192, 227], P(None, ('nodes', 'feat')), may hold values from -6 to 6
- area_weight: float32 [4, 8192], P(None, ('nodes', 'feat')), may hold values from 0.2 to 1
- grid_count: int32 [4, 16], P(None, 'nodes'), may hold values from 1 to 512, as said below
- g2m_edges: int32 [2, 32768], P(None, 'nodes'), may hold values from 0 to 1535, as said below
- mesh_edges: int32 [2, 81920], P(None, 'nodes'), may hold values from 0 to 1919, as said below
- m2g_edges: int32 [2, 49152], P(None, 'nodes'), may hold values from 0 to 1919, as said below
- edge_count: int32 [3, 16], P(None, 'nodes'), may hold values from 1024 to 5120, as said below
- embed_weight: float32 [227, 512], P(None, ('nodes', 'feat')), may hold values from -0.375 to 0.375
- embed_first: float32 [227, 512], P(None, ('nodes', 'feat')), may hold values from -0.0017089844 to 0.0017089844
- embed_second: float32 [227, 512], P(None, ('nodes', 'feat')), may hold values from 5.452073e-08 to 2.1487583e-07
- node_mats: float32 [11, 512, 512], P(None, ('nodes', 'feat')), may hold values from -0.25 to 0.25
- mats_first: float32 [11, 512, 512], P(None, ('nodes', 'feat')), may hold values from -0.0017089844 to 0.0017089844
- mats_second: float32 [11, 512, 512], P(None, ('nodes', 'feat')), may hold values from 5.452073e-08 to 2.1487583e-07
- head_weight: float32 [512, 227], P(('nodes', 'feat')), may hold values from -0.25 to 0.25
- head_first: float32 [512, 227], P(('nodes', 'feat')), may hold values from -0.0017089844 to 0.0017089844
- head_second: float32 [512, 227], P(('nodes', 'feat')), may hold values from 5.452073e-08 to 2.1487583e-07
- norm_gains: float32 [4, 512], P(None, ('nodes', 'feat'))
- gains_first: float32 [4, 512], P(None, ('nodes', 'feat')), may hold values from -0.0068359375 to 0.0068359375
- gains_second: float32 [4, 512], P(None, ('nodes', 'feat')), may hold values from 8.659175e-07 to 3.431599e-06
Outputs:
- loss_sum: float32 [], replicated
- weight_sum: float32 [], replicated
- grad_norm: float32 [], replicated
- embed_new: float32 [227, 512], P(None, ('nodes', 'feat'))
- embed_moment: float32 [227, 512], P(None, ('nodes', 'feat'))
- embed_square: float32 [227, 512], P(None, ('nodes', 'feat'))
- embed_copy: bfloat16 [227, 512], P(None, ('nodes', 'feat'))
- mats_new: float32 [11, 512, 512], P(None, ('nodes', 'feat'))
- mats_moment: float32 [11, 512, 512], P(None, ('nodes', 'feat'))
- mats_square: float32 [11, 512, 512], P(None, ('nodes', 'feat'))
- mats_copy: bfloat16 [11, 512, 512], P(None, ('nodes', 'feat'))
- head_new: float32 [512, 227], P(('nodes', 'feat'))
- head_moment: float32 [512, 227], P(('nodes', 'feat'))
- head_square: float32 [512, 227], P(('nodes', 'feat'))
- head_copy: bfloat16 [512, 227], P(('nodes', 'feat'))
- gains_new: float32 [4, 512], P(None, ('nodes', 'feat'))
- gains_moment: float32 [4, 512], P(None, ('nodes', 'feat'))
- gains_square: float32 [4, 512], P(None, ('nodes', 'feat'))
- gains_copy: bfloat16 [4, 512], P(None, ('nodes', 'feat'))
Inputs may be any that keep to these rules, and one draw needn't show every extreme that they name: `grid_count`: each block's live cell slots are a prefix of its 512 slots; the last block has all of them live. `g2m_edges`: row 0 is a sender in rim coordinates: 0 to 511 the previous block (wrapping), 512 to 1023 the own block, then the next block; row 1 is a mesh node of the own block. `mesh_edges`: row 0 is a mesh sender in rim coordinates over the previous, own and next blocks of 640; row 1 a mesh node of the own block. `m2g_edges`: row 0 is a mesh sender in rim coordinates over the previous, own and next blocks of 640; row 1 a cell of the own block. `edge_count`: row 0 counts g2m slots (at most 2048), row 1 mesh slots (at most 5120), row 2 m2g slots (at most 3072); live slots are a prefix, at least half of a block's slots, and in each row some block has all slots live.
All inputs are finite; a program needn't handle non-finite values.
Results may differ from a plain program's by a relative error of at most 0.0044.
The roundings to bfloat16 on the way count: a program that leaves them out, or rounds other values in their place, can miss the bound.
Values may be sent and summed in bfloat16 or wider, within the bound.
A program may use at most 256 MiB of HBM per device.

v0:
```python
import functools
import math

import jax
import jax.numpy as jnp
from jax import lax
from jax.experimental import pallas as pl
from jax.experimental.pallas import tpu as pltpu
from jax.sharding import PartitionSpec as P

M_DEV = 640
STEP = 5
MICRO = 4


EPS_NORM = 1e-05
CLIP = 0.5
RATE = 0.04
GAIN_RATE = 0.4
BETA_ONE = 0.5
BETA_TWO = 0.6
EPS_ADAM = 1e-08
DECAY = 0.1

BOTH = ("nodes", "feat")


def matmul(a, b):
    return jnp.dot(a, b, preferred_element_type=jnp.float32)


def left_dot(a, b):
    return lax.dot_general(a, b, (((0,), (0,)), ((), ())), preferred_element_type=jnp.float32)


def right_dot(a, b):
    return lax.dot_general(a, b, (((1,), (1,)), ((), ())), preferred_element_type=jnp.float32)


class Plan:
    def __init__(self, nodes):
        self.nodes = nodes
        self.chips = nodes // MICRO
        self.bits = self.chips.bit_length() - 1
        width = math.isqrt(self.chips)
        self.width = width if width * width == self.chips else 0

    def device(self, m, j, c):
        return (m * self.chips + walk(j % self.chips, self.width)) * 2 + c

    def ring(self, step):
        pairs = []
        length = 2 * self.chips
        for m in range(MICRO):
            for q in range(length):
                to = (q + step) % length
                pairs.append((self.device(m, q // 2, q % 2), self.device(m, to // 2, to % 2)))
        return pairs


MESH = pl.DeviceIdType.MESH
CODE_BITS = 12


def walk(value, width):
    if width == 0:
        return value
    row, col = value // width, value % width
    return row * width + col + (row % 2) * (width - 1 - 2 * col)


class Spot:
    def __init__(self, plan):
        me = lax.axis_index("nodes")
        self.plan = plan
        self.core = lax.axis_index("feat")
        self.z = me // plan.chips
        self.p = me % plan.chips

    def bit(self, b):
        return (self.p // (1 << b)) % 2

    def peer_z(self, d):
        return {"nodes": ((self.z + d) % MICRO) * self.plan.chips + self.p, "feat": self.core}

    def peer_bit(self, b):
        other = self.p + (1 - 2 * self.bit(b)) * (1 << b)
        return {"nodes": self.z * self.plan.chips + other, "feat": self.core}

    def in_plane(self, p, core):
        return {"nodes": self.z * self.plan.chips + p, "feat": core}

    def sibling(self):
        return self.in_plane(self.p, 1 - self.core)

    def partners(self):
        chips = self.plan.chips
        found = [self.peer_z(d) for d in range(1, MICRO)]
        for turn in range(chips):
            p = (self.p + turn) % chips
            if turn:
                found.append(self.in_plane(p, self.core))
            found.append(self.in_plane(p, 1 - self.core))
        return found

    def meet(self):
        barrier = pltpu.get_barrier_semaphore()
        found = self.partners()
        for other in found:
            pl.semaphore_signal(barrier, inc=1, device_id=other, device_id_type=MESH)
        pl.semaphore_wait(barrier, len(found))

    def held(self, done):
        bits = range(self.plan.bits - 1, -1, -1)
        return tuple(slice(None) if b in done else self.bit(b) for b in bits)


def remote(src, dst, send, recv, to):
    return pltpu.make_async_remote_copy(
        src_ref=src, dst_ref=dst, send_sem=send, recv_sem=recv, device_id=to, device_id_type=MESH
    )


def gather_kernel(
    plan,
    shapes,
    pack_ref,
    cells_ref,
    codes_ref,
    all_ref,
    main_ref,
    halo_ref,
    enc_ref,
    proc_ref,
    dec_ref,
    graph_ref,
    total,
    whole,
    cell_hop,
    code_hop,
    own_sem,
    out_sem,
    hop_send,
    hop_recv,
    plane_send,
    plane_recv,
    twin_send,
    twin_recv,
    move_send,
    move_recv,
):
    spot = Spot(plan)
    z, p, core = spot.z, spot.p, spot.core
    chips, bits = plan.chips, plan.bits
    groups = bits
    mats = pack_ref.shape[0] // groups
    code_rows = codes_ref.shape[0] // 2
    lanes = halo_ref.shape[-1]
    own = pltpu.make_async_copy(pack_ref, all_ref.at[(slice(None), z) + spot.held(()) + (core,)], own_sem)
    own.start()
    spot.meet()
    my_codes = codes_ref.at[pl.ds(pl.multiple_of(core * code_rows, 8), code_rows)]
    hops = []
    for d in range(1, MICRO):
        to = spot.peer_z(d)
        m = (z + d) % MICRO
        for n, (src, dst) in enumerate(
            (
                (my_codes, code_hop.at[d - 1]),
                (cells_ref.at[m], cell_hop.at[d - 1]),
                (pack_ref, all_ref.at[(slice(None), z) + spot.held(()) + (core,)]),
            )
        ):
            copy = remote(src, dst, hop_send.at[d - 1, n], hop_recv.at[d - 1, n], to)
            copy.start()
            hops.append(copy)
    quarter = p % 4
    bb, to_core = quarter % 2, quarter // 2
    slot = bb * 2 + core
    half_slot = (1 - bb) * 2 + core
    moves = []

    def move(d, n, src, dst, sem, chip, to_core):
        here = jnp.logical_and(chip == p, to_core == core)
        copy = remote(src, dst, move_send.at[d, n], sem, spot.in_plane(chip, to_core))

        @pl.when(here)
        def _():
            pltpu.make_async_copy(src, dst, sem).start()

        @pl.when(jnp.logical_not(here))
        def _():
            copy.start()

        moves.append((here, copy))

    def spread_codes(d):
        block = ((z - d) % MICRO) * chips + p
        codes = my_codes if d == 0 else code_hop.at[d - 1]
        rows = pl.ds(pl.multiple_of(core * code_rows, 8), code_rows)
        dst = graph_ref.at[bb, rows]
        move(d, 0, codes, dst, move_recv.at[0, slot], walk(block // 4, plan.width), to_core)

    def spread(d):
        block = ((z - d) % MICRO) * chips + p
        j = block // 4
        chip = walk(j, plan.width)
        q = (2 * j + to_core + 2 * bb - 1) % (2 * chips)
        near = walk(q // 2, plan.width)
        cells = cells_ref.at[z] if d == 0 else cell_hop.at[d - 1]
        move(
            d,
            1,
            cells.at[:, pl.ds(0, lanes)],
            halo_ref.at[1 - bb, core],
            move_recv.at[1, half_slot],
            near,
            q % 2,
        )
        move(d, 2, cells, main_ref.at[bb, core], move_recv.at[2, slot], chip, to_core)

    def region(d, done):
        return ((z - d) % MICRO,) + spot.held(done) + (core,)

    planes = {}

    def step(d, g, t):
        done = tuple((g + s) % bits for s in range(t))
        where = (pl.ds(g * mats, mats),) + region(d, done)
        copy = remote(
            all_ref.at[where],
            all_ref.at[where],
            plane_send.at[d, g, t],
            plane_recv.at[d, g, t],
            spot.peer_bit((g + t) % bits),
        )
        copy.start()
        planes[d, g, t] = copy

    for d in range(MICRO):
        if d:
            hops[3 * (d - 1)].wait_recv()
        spread_codes(d)
    outs = []

    def build(n, side_block):
        first, edges, rows, columns = shapes[n]
        chunk = math.gcd(edges, 1024) // 128
        area = (pl.ds(0, rows), pl.ds(0, columns))

        def ones(row, count):
            place = lax.broadcasted_iota(jnp.int32, (count, 128), 0).astype(jnp.int16)
            hit = place == row.astype(jnp.int16)
            return jnp.where(hit, jnp.bfloat16(1), jnp.bfloat16(0)).astype(jnp.float8_e4m3fn)

        def body(k, _):
            into, out = [], []
            for i in range(chunk):
                code = graph_ref[side_block, pl.ds(first + k * chunk + i, 1), :]
                into.append(ones(code >> CODE_BITS, rows))
                out.append(ones(code & ((1 << CODE_BITS) - 1), columns))
            total[area] += right_dot(jnp.concatenate(into, axis=1), jnp.concatenate(out, axis=1))
            return 0

        total[area] = jnp.zeros((rows, columns), jnp.float32)
        lax.fori_loop(0, edges // (128 * chunk), body, 0)
        if len(outs) >= 2:
            outs[-2].wait()
        side = len(outs) % 2
        whole[(side,) + area] = total[area].astype(jnp.bfloat16)
        ref = (enc_ref, proc_ref, dec_ref)[n]
        copy = pltpu.make_async_copy(whole.at[(side,) + area], ref.at[side_block], out_sem.at[side])
        copy.start()
        outs.append(copy)

    work = [[], [(0, 0), (0, 1)], [(1, 0)], [(1, 1)], [(2, 0)], [(2, 1)]]
    twins = []
    for tick in range(MICRO + bits):
        for t in range(bits + 1):
            d = tick - t
            if d < 0 or d >= MICRO:
                continue
            if t == 0:
                if d == 0:
                    own.wait()
                else:
                    hops[3 * (d - 1) + 1].wait_recv()
                    hops[3 * (d - 1) + 2].wait_recv()
                spread(d)
            else:
                for g in range(groups):
                    planes[d, g, t - 1].wait_recv()
            if t < bits:
                for g in range(groups):
                    step(d, g, t)
            else:
                where = (slice(None),) + region(d, tuple(range(bits)))
                copy = remote(
                    all_ref.at[where], all_ref.at[where], twin_send.at[d], twin_recv.at[d], spot.sibling()
                )
                copy.start()
                twins.append(copy)
        if tick == 1:
            for n in range(4):
                dst = graph_ref.at[n // 2, pl.ds((n % 2) * code_rows, code_rows)]
                pltpu.make_async_copy(dst, dst, move_recv.at[0, n]).wait()
        for kind, block in work[tick] if tick < len(work) else []:
            build(kind, block)
    for copy in outs[-2:]:
        copy.wait()
    for copy in hops + list(planes.values()):
        copy.wait_send()
    for copy in twins:
        copy.wait()
    for here, copy in moves:

        @pl.when(jnp.logical_not(here))
        def _():
            copy.wait_send()

    for n in range(4):
        half, side = n % 2, n // 2
        for kind, dst in ((1, halo_ref.at[side, half]), (2, main_ref.at[side, half])):
            pltpu.make_async_copy(dst, dst, move_recv.at[kind, n]).wait()


def gather_all(plan, shapes, pack, cells, codes):
    mats, rows, width = pack.shape
    micro, half, lanes = cells.shape
    bits = plan.bits
    most_rows = max(shape[2] for shape in shapes)
    most_columns = max(shape[3] for shape in shapes)
    any_space = pl.BlockSpec(memory_space=pl.ANY)
    dma = pltpu.SemaphoreType.DMA
    return pl.pallas_call(
        functools.partial(gather_kernel, plan, shapes),
        out_shape=(
            jax.ShapeDtypeStruct((mats, MICRO) + (2,) * bits + (2, rows, width), pack.dtype),
            jax.ShapeDtypeStruct((2, 2, half, lanes), cells.dtype),
            jax.ShapeDtypeStruct((2, 2, half, lanes // 2), cells.dtype),
            *(jax.ShapeDtypeStruct((2,) + shape[2:], jnp.bfloat16) for shape in shapes),
        ),
        in_specs=[any_space] * 3,
        out_specs=(any_space,) * 6,
        scratch_shapes=[
            pltpu.VMEM((2,) + codes.shape, codes.dtype),
            pltpu.VMEM((most_rows, most_columns), jnp.float32),
            pltpu.VMEM((2, most_rows, most_columns), jnp.bfloat16),
            pltpu.VMEM((MICRO - 1, half, lanes), cells.dtype),
            pltpu.VMEM((MICRO - 1, codes.shape[0] // 2, codes.shape[1]), codes.dtype),
            dma,
            dma((2,)),
            dma((MICRO - 1, 3)),
            dma((MICRO - 1, 3)),
            dma((MICRO, bits, bits)),
            dma((MICRO, bits, bits)),
            dma((MICRO,)),
            dma((MICRO,)),
            dma((MICRO, 3)),
            dma((3, 4)),
        ],
        compiler_params=pltpu.CompilerParams(
            collective_id=0, has_side_effects=True, vmem_limit_bytes=48 << 20
        ),
        name="gather_all",
    )(pack, cells, codes)


def reduce_kernel(
    plan,
    grads_ref,
    low_ref,
    stats_ref,
    share_ref,
    total_ref,
    acc,
    twin_in,
    plane_out,
    plane_in,
    hop_out,
    hop_in,
    z_stats,
    plane_stats,
    twin_stats,
    own_sem,
    twin_send,
    twin_recv,
    plane_send,
    plane_recv,
    hop_send,
    hop_recv,
    stat_send,
    stat_recv,
):
    spot = Spot(plan)
    z, p, core = spot.z, spot.p, spot.core
    chips, bits = plan.chips, plan.bits
    groups = bits
    mats = grads_ref.shape[0]
    part = mats // groups
    every = (slice(None),) * bits
    order = [1, 2, 3, 0]
    owns = {}
    for d in order:
        item = (z + d) % MICRO
        owns[d] = pltpu.make_async_copy(
            grads_ref.at[(slice(None), item) + every + (core,)], acc.at[d], own_sem.at[d]
        )
        owns[d].start()
    spot.meet()
    twins = {}
    for d in order:
        item = (z + d) % MICRO
        twins[d] = remote(
            low_ref.at[(slice(None), item) + every + (1 - core,)],
            twin_in.at[d],
            twin_send.at[d],
            twin_recv.at[d],
            spot.sibling(),
        )
        twins[d].start()

    def starts(t):
        return sum(1 << (bits - 1 - s) for s in range(t))

    planes, hops = {}, []

    def send_step(d, g, t):
        done = tuple((g + s) % bits for s in range(t))
        b = (g + t) % bits
        count = 1 << (bits - 1 - t)
        at = starts(t)
        theirs = tuple(
            spot.bit(n) if n in done else (1 - spot.bit(n) if n == b else slice(None))
            for n in range(bits - 1, -1, -1)
        )

        def body(n, _):
            mat = g * part + n
            value = acc[(d, mat) + theirs]
            plane_out[d, mat, at : at + count] = value.reshape((count,) + value.shape[-2:]).astype(
                plane_out.dtype
            )
            return 0

        lax.fori_loop(0, part, body, 0)
        where = (d, pl.ds(g * part, part), pl.ds(at, count))
        planes[d, g, t] = remote(
            plane_out.at[where],
            plane_in.at[where],
            plane_send.at[d, g, t],
            plane_recv.at[d, g, t],
            spot.peer_bit(b),
        )
        planes[d, g, t].start()

    def add_step(d, g, t):
        planes[d, g, t].wait_recv()
        done = tuple((g + s) % bits for s in range(t + 1))
        count = 1 << (bits - 1 - t)
        at = starts(t)
        mine = tuple(spot.bit(n) if n in done else slice(None) for n in range(bits - 1, -1, -1))

        def body(n, _):
            mat = g * part + n
            where = (d, mat) + mine
            value = acc[where]
            came = plane_in[d, mat, at : at + count].astype(jnp.float32)
            acc[where] = value + came.reshape(value.shape)
            return 0

        lax.fori_loop(0, part, body, 0)

    for tick in range(MICRO + bits):
        for t in range(bits + 1):
            n = tick - t
            if n < 0 or n >= MICRO:
                continue
            d = order[n]
            if t == 0:
                owns[d].wait()
                twins[d].wait_recv()

                def body(mat, _):
                    acc[d, mat] = acc[d, mat] + twin_in[d, mat].astype(jnp.float32)
                    return 0

                lax.fori_loop(0, mats, body, 0)
            else:
                for g in range(groups):
                    add_step(d, g, t - 1)
            if t < bits:
                for g in range(groups):
                    send_step(d, g, t)
            elif d:

                def body(mat, _):
                    hop_out[d - 1, mat] = acc[(d, mat) + spot.held(())].astype(hop_out.dtype)
                    return 0

                lax.fori_loop(0, mats, body, 0)
                copy = remote(
                    hop_out.at[d - 1], hop_in.at[d - 1], hop_send.at[d - 1], hop_recv.at[d - 1], spot.peer_z(d)
                )
                copy.start()
                hops.append(copy)
    for copy in hops:
        copy.wait_recv()

    def body(mat, square):
        value = acc[(0, mat) + spot.held(())]
        for d in range(MICRO - 1):
            value = value + hop_in[d, mat].astype(jnp.float32)
        share_ref[mat] = value
        return square + value * value

    square = lax.fori_loop(0, mats, body, jnp.zeros(share_ref.shape[1:], jnp.float32))
    square = jnp.sum(square, axis=0, keepdims=True)
    lanes = total_ref.shape[1]
    square = sum(square[:, n : n + lanes] for n in range(0, square.shape[1], lanes))
    row = lax.broadcasted_iota(jnp.int32, total_ref.shape, 0)
    tile = jnp.where(row == 0, square, stats_ref[...])
    sends = []

    def exchange(buffer, index, targets, at):
        buffer[index] = tile
        copies = []
        for n, to in enumerate(targets):
            copy = remote(
                buffer.at[index], buffer.at[index], stat_send.at[at + n], stat_recv.at[at + n], to
            )
            copy.start()
            copies.append(copy)
        for copy in copies:
            copy.wait()
        total = buffer[0]
        for n in range(1, buffer.shape[0]):
            total = total + buffer[n]
        return total

    tile = exchange(z_stats, z, [spot.peer_z(d) for d in range(1, MICRO)], 0)
    tile = exchange(
        plane_stats, p, [spot.in_plane((p + d) % chips, core) for d in range(1, chips)], MICRO - 1
    )
    tile = exchange(twin_stats, core, [spot.sibling()], MICRO + chips - 2)
    total_ref[...] = tile
    for copy in list(twins.values()) + list(planes.values()) + hops:
        copy.wait_send()


def reduce_all(plan, grads, low, stats):
    mats, rows, width = grads.shape[0], grads.shape[-2], grads.shape[-1]
    bits, chips = plan.bits, plan.chips
    shards = (2,) * bits
    steps = chips - 1
    any_space = pl.BlockSpec(memory_space=pl.ANY)
    vmem = pl.BlockSpec(memory_space=pltpu.VMEM)
    dma = pltpu.SemaphoreType.DMA
    return pl.pallas_call(
        functools.partial(reduce_kernel, plan),
        out_shape=(
            jax.ShapeDtypeStruct((mats, rows, width), jnp.float32),
            jax.ShapeDtypeStruct(stats.shape, jnp.float32),
        ),
        in_specs=[any_space, any_space, vmem],
        out_specs=(vmem, vmem),
        scratch_shapes=[
            pltpu.VMEM((MICRO, mats) + shards + (rows, width), jnp.float32),
            pltpu.VMEM((MICRO, mats) + shards + (rows, width), low.dtype),
            pltpu.VMEM((MICRO, mats, steps, rows, width), jnp.bfloat16),
            pltpu.VMEM((MICRO, mats, steps, rows, width), jnp.bfloat16),
            pltpu.VMEM((MICRO - 1, mats, rows, width), jnp.bfloat16),
            pltpu.VMEM((MICRO - 1, mats, rows, width), jnp.bfloat16),
            pltpu.VMEM((MICRO,) + stats.shape, jnp.float32),
            pltpu.VMEM((chips,) + stats.shape, jnp.float32),
            pltpu.VMEM((2,) + stats.shape, jnp.float32),
            dma((MICRO,)),
            dma((MICRO,)),
            dma((MICRO,)),
            dma((MICRO, bits, bits)),
            dma((MICRO, bits, bits)),
            dma((MICRO - 1,)),
            dma((MICRO - 1,)),
            dma((MICRO + chips - 1,)),
            dma((MICRO + chips - 1,)),
        ],
        compiler_params=pltpu.CompilerParams(
            collective_id=1, has_side_effects=True, vmem_limit_bytes=56 << 20
        ),
        name="reduce_all",
    )(grads, low, stats)


def norm_rows(z, gain):
    mean = jnp.mean(z, axis=-1, keepdims=True)
    centred = z - mean
    spread = jnp.mean(centred * centred, axis=-1, keepdims=True)
    return centred * lax.rsqrt(spread + EPS_NORM) * gain


def update_fwd(index, base, agg, mats, gains):
    pre = matmul(agg, mats[index])
    if base is not None:
        pre = pre + matmul(base, mats[3 + index])
    active = jax.nn.silu(pre).astype(jnp.bfloat16)
    inner = matmul(active, mats[7 + index])
    return (norm_rows(inner, gains[index]), (pre, active, inner))


def update_bwd(index, base, agg, mats, gains, kept, grad_out):
    pre, active, inner = kept
    _, pull = jax.vjp(norm_rows, inner, gains[index])
    grad_inner, grad_gain = pull(grad_out)
    inner_low = grad_inner.astype(jnp.bfloat16)
    grad_second = left_dot(active, inner_low)
    grad_active = right_dot(inner_low, mats[7 + index])
    sigma = jax.nn.sigmoid(pre)
    pre_low = (grad_active * sigma * (1.0 + pre * (1.0 - sigma))).astype(jnp.bfloat16)
    grad_first = left_dot(agg, pre_low)
    grad_agg = right_dot(pre_low, mats[index])
    grad_self = None
    grad_base = None
    if base is not None:
        grad_self = left_dot(base, pre_low)
        grad_base = right_dot(pre_low, mats[3 + index])
    return (grad_base, grad_agg, grad_first, grad_self, grad_second, grad_gain)


def adamw(param, first, second, grad, scale, rate):
    clipped = grad * scale
    moment = BETA_ONE * first + (1.0 - BETA_ONE) * clipped
    square = BETA_TWO * second + (1.0 - BETA_TWO) * clipped * clipped
    fixed_one = moment / (1.0 - BETA_ONE**STEP)
    fixed_two = square / (1.0 - BETA_TWO**STEP)
    fresh = param - rate * (fixed_one / (jnp.sqrt(fixed_two) + EPS_ADAM) + DECAY * param)
    return (fresh, moment, square, fresh.astype(jnp.bfloat16))


def on_device(
    plan,
    grid_in,
    targets,
    area_weight,
    grid_count,
    g2m_edges,
    mesh_edges,
    m2g_edges,
    edge_count,
    embed_weight,
    embed_first,
    embed_second,
    node_mats,
    mats_first,
    mats_second,
    head_weight,
    head_first,
    head_second,
    norm_gains,
    gains_first,
    gains_second,
):
    half, variables = grid_in.shape[1:]
    grid_rows = 2 * half
    mesh_rows = M_DEV
    lanes = -(-variables // 128) * 128
    core = lax.axis_index("feat")

    position = core * half + jnp.arange(half, dtype=jnp.int32)
    weights = jnp.where(position[None, :] < grid_count, area_weight, 0.0)
    pieces = []
    rest = weights
    for _ in range(3):
        piece = lax.reduce_precision(rest, 8, 7)
        pieces.append(piece.astype(jnp.bfloat16))
        rest = rest - piece
    cells = jnp.concatenate(
        [
            jnp.pad(grid_in, ((0, 0), (0, 0), (0, lanes - variables))),
            targets,
            jnp.pad(jnp.stack(pieces, axis=-1), ((0, 0), (0, 0), (0, lanes - variables - 3))),
        ],
        axis=-1,
    )
    last = jnp.concatenate(
        [
            jnp.pad(embed_weight.T, ((0, 0), (0, lanes - variables))),
            head_weight,
            jnp.pad(norm_gains.T, ((0, 0), (0, lanes - variables - 4))),
        ],
        axis=-1,
    )
    pack = jnp.concatenate([node_mats, last[None]]).astype(jnp.bfloat16)
    graphs = ((g2m_edges, grid_rows, mesh_rows), (mesh_edges, mesh_rows, mesh_rows), (m2g_edges, mesh_rows, grid_rows))
    codes, shapes = [], []
    first = 0
    for n, (edges, columns, rows) in enumerate(graphs):
        per = edges.shape[1]
        alive = jnp.arange(per, dtype=jnp.int32) < edge_count[n, 0]
        codes.append(jnp.where(alive, edges[1] * (1 << CODE_BITS) + edges[0], -1))
        shapes.append((first // 128, per, rows, 3 * columns))
        first += per
    codes = jnp.concatenate(codes).reshape(-1, 128)
    gathered, main, halo, encoder, processor, decoder = gather_all(plan, shapes, pack, cells, codes)
    width = pack.shape[2]
    full = gathered.reshape(-1, width, width)
    mats = full[:-1]
    embed = full[-1, :, :lanes]
    head = full[-1, :, lanes:]
    gains = full[-1, :, lanes + variables : lanes + variables + 4].T.astype(jnp.float32)
    main = main.reshape(-1, 2 * lanes)
    inputs = main[:, :lanes]
    wanted = main[:, lanes:]
    weight = sum(
        main[:, lanes + variables + n : lanes + variables + n + 1].astype(jnp.float32) for n in range(3)
    )
    halo = halo.reshape(2, grid_rows, lanes)
    inputs_ext = jnp.concatenate([halo[0], inputs, halo[1]])
    def extended(rows):
        size = rows.shape[0] // 2
        before = lax.ppermute(rows[size:], BOTH, plan.ring(1))
        after = lax.ppermute(rows[:size], BOTH, plan.ring(-1))
        return jnp.concatenate([before, rows, after])

    def collect(graph, ext):
        size = ext.shape[0] // 4
        return jnp.concatenate(
            [matmul(graph[b], ext[b * size : (b + 3) * size]) for b in range(2)]
        ).astype(jnp.bfloat16)

    def collect_back(graph, grad_agg):
        low = grad_agg.astype(jnp.bfloat16)
        size = low.shape[0] // 2
        pieces = [left_dot(graph[b], low[b * size : (b + 1) * size]) for b in range(2)]
        rows = pieces[0].shape[0] // 3
        before = pieces[0][:rows].astype(jnp.bfloat16)
        after = pieces[1][2 * rows :].astype(jnp.bfloat16)
        from_right = lax.ppermute(before, BOTH, plan.ring(-1)).astype(jnp.float32)
        from_left = lax.ppermute(after, BOTH, plan.ring(1)).astype(jnp.float32)
        first = from_left + pieces[0][rows : 2 * rows] + pieces[1][:rows]
        second = pieces[0][2 * rows :] + pieces[1][rows : 2 * rows] + from_right
        return jnp.concatenate([first, second]).astype(jnp.bfloat16).astype(jnp.float32)

    hidden_ext = right_dot(inputs_ext, embed)
    grid_hidden = hidden_ext[grid_rows : 3 * grid_rows]
    low_ext = hidden_ext.astype(jnp.bfloat16)
    grid_low = low_ext[grid_rows : 3 * grid_rows]
    aggs = [collect(encoder, low_ext)]
    nodes, kept_first = update_fwd(0, None, aggs[0], mats, gains)
    kept = [kept_first]
    lows = [None]
    for index in (1, 2):
        mesh_low = nodes.astype(jnp.bfloat16)
        lows.append(mesh_low)
        aggs.append(collect(processor, extended(mesh_low)))
        branch, kept_now = update_fwd(index, mesh_low, aggs[index], mats, gains)
        kept.append(kept_now)
        nodes = nodes + branch
    aggs.append(collect(decoder, extended(nodes.astype(jnp.bfloat16))))
    branch, kept_now = update_fwd(3, grid_low, aggs[3], mats, gains)
    kept.append(kept_now)
    out_low = (grid_hidden + branch).astype(jnp.bfloat16)
    error = matmul(out_low, head) - wanted.astype(jnp.float32)
    error = jnp.where(jnp.arange(lanes) < variables, error, 0.0)
    loss_local = jnp.sum(weight * error * error)
    weight_local = jnp.sum(weight)
    grad_pred = (2.0 * weight * error).astype(jnp.bfloat16)
    grad_head = left_dot(out_low, grad_pred)
    grad_grid = right_dot(grad_pred, head)
    pieces = [None] * 11
    gain_grads = [None] * 4
    grad_base, grad_agg, pieces[3], pieces[6], pieces[10], gain_grads[3] = update_bwd(
        3, grid_low, aggs[3], mats, gains, kept[3], grad_grid
    )
    grad_grid = grad_grid + grad_base
    grad_nodes = collect_back(decoder, grad_agg)
    for index in (2, 1):
        (
            grad_base,
            grad_agg,
            pieces[index],
            pieces[3 + index],
            pieces[7 + index],
            gain_grads[index],
        ) = update_bwd(index, lows[index], aggs[index], mats, gains, kept[index], grad_nodes)
        grad_nodes = grad_nodes + grad_base + collect_back(processor, grad_agg)
    _, grad_agg, pieces[0], _, pieces[7], gain_grads[0] = update_bwd(
        0, None, aggs[0], mats, gains, kept[0], grad_nodes
    )
    grad_grid = grad_grid + collect_back(encoder, grad_agg)
    grad_embed = left_dot(grad_grid.astype(jnp.bfloat16), inputs)
    gain_part = jnp.pad(jnp.stack(gain_grads).T, ((0, 0), (variables, lanes - variables - 4)))
    pieces.append(jnp.concatenate([grad_embed, grad_head + gain_part], axis=1))
    grads = jnp.stack(pieces).reshape(gathered.shape)
    row = jnp.arange(8)[:, None]
    stats = jnp.where(row == 1, loss_local, jnp.where(row == 2, weight_local, 0.0))
    stats = jnp.where(jnp.arange(128)[None, :] == 0, stats, 0.0)
    share, total = reduce_all(plan, grads, grads.astype(jnp.bfloat16), stats)
    square_sum, loss_sum, weight_sum = (jnp.sum(total[n]) for n in range(3))
    shares = (
        share[-1, :, :variables].T,
        share[:-1],
        share[-1, :, lanes : lanes + variables],
        share[-1, :, lanes + variables : lanes + variables + 4].T,
    )
    grad_norm = jnp.sqrt(square_sum)
    scale = jnp.minimum(1.0, CLIP / (grad_norm + 1e-06))
    return (
        loss_sum,
        weight_sum,
        grad_norm,
        *adamw(embed_weight, embed_first, embed_second, shares[0], scale, RATE),
        *adamw(node_mats, mats_first, mats_second, shares[1], scale, RATE),
        *adamw(head_weight, head_first, head_second, shares[2], scale, RATE),
        *adamw(norm_gains, gains_first, gains_second, shares[3], scale, GAIN_RATE),
    )


def solution(mesh):
    plan = Plan(mesh.shape["nodes"])
    cells = P(None, BOTH, None)
    columns = P(None, BOTH)
    rows = P(BOTH, None)
    blocks = P(None, "nodes")
    return jax.shard_map(
        lambda *args: on_device(plan, *args),
        mesh=mesh,
        in_specs=(
            (cells, cells, columns, blocks, blocks, blocks, blocks, blocks)
            + (columns,) * 3
            + (cells,) * 3
            + (rows,) * 3
            + (columns,) * 3
        ),
        out_specs=(P(), P(), P()) + (columns,) * 4 + (cells,) * 4 + (rows,) * 4 + (columns,) * 4,
        check_vma=False,
    )
```

profile of v0, /device:TPU:0, one launch (start us, length us, event | category | flops | bytes accessed | tf_op | source)
XLA Modules:
  0.0 383.3 jit_solution(2257109073292004021)
XLA Ops:
  10.8 78.5 %gather_all.1 = (bf16[12,4,2,2,2,16,512]{6,5,4,3,2,1,0:T(8,128)(2,1)}, bf16[2,2,256,512]{3,2,1,0:T(8,128)(2,1)S(1)}, bf16[2,2,256,256]{3,2,1,0:T(8,128)(2,1)S(1)...) custom-call(bf16[12,16,512]{2,1,0:T(8,128)(2,1)S(1)} %pad_maximum_fusion.14.pack_ref, ...), custom_call_target="tpu_custom_call" | custom-call | tf_op jit(solution)/shard_map/gather_all/pallas_call | solution.py:335
  89.4 3.8 fusion.236
  97.2 1.9 fusion.229
  99.2 2.7 multiply_convert_fusion.2
  105.1 2.2 multiply_convert_fusion.3
  107.5 1.9 collective-permute-start.1
  109.4 8.1 %collective-permute-done = bf16[640,512]{1,0:T(8,128)(2,1)S(1)} collective-permute-done((bf16[640,512]{1,0:T(8,128)(2,1)S(1)}, bf16[640,512]{1,0:T(8,128)(2,1)S(1)}, u32[]{:S(2)}, u32[]{:S(2)}) %collective-permute-start) | collective-permute-done | bytes 655392 | tf_op jit(solution)/shard_map/ppermute | solution.py:720
  117.5 3.3 fusion.94
  123.2 2.6 multiply_convert_fusion.1
  128.9 2.3 fusion.228
  131.2 2.6 collective-permute-start.2
  133.8 7.5 %collective-permute-done.2 = bf16[640,512]{1,0:T(8,128)(2,1)S(1)} collective-permute-done((bf16[640,512]{1,0:T(8,128)(2,1)S(1)}, bf16[640,512]{1,0:T(8,128)(2,1)S(1)}, u32[]{:S(2)}, u32[]{:S(2)}) %collective-permute-start.2) | collective-permute-done | bytes 655392 | tf_op jit(solution)/shard_map/ppermute | solution.py:720
  145.7 2.7 multiply_convert_fusion
  148.3 2.4 fusion.239
  150.8 3.2 copy.146
  154.0 2.4 multiply_reduce_fusion.4
  156.5 2.4 add_convert_fusion.3
  159.0 3.5 collective-permute-start.4
  163.8 5.2 %collective-permute-done.4 = bf16[640,512]{1,0:T(8,128)(2,1)S(1)} collective-permute-done((bf16[640,512]{1,0:T(8,128)(2,1)S(1)}, bf16[640,512]{1,0:T(8,128)(2,1)S(1)}, u32[]{:S(2)}, u32[]{:S(2)}) %collective-permute-start.4) | collective-permute-done | bytes 655392 | tf_op jit(solution)/shard_map/ppermute | solution.py:720
  174.1 2.3 multiply_convert_fusion.5
  176.4 2.1 fusion.240
  178.5 1.9 copy.147
  180.9 2.0 fusion.28
  183.9 2.0 fusion.133
  186.9 2.8 fusion.172
  189.6 2.9 copy.148
  192.6 2.4 multiply_reduce_fusion.7
  202.7 2.2 collective-permute-start.7
  210.5 2.5 collective-permute-done.7
  213.0 2.6 collective-permute-done.6
  216.4 2.0 fusion.11
  218.5 2.3 fusion.226
  223.2 1.7 fusion.22
  225.0 1.7 fusion.14
  230.9 4.0 %collective-permute-done.9 = bf16[640,512]{1,0:T(8,128)(2,1)S(1)} collective-permute-done((bf16[640,512]{1,0:T(8,128)(2,1)S(1)}, bf16[640,512]{1,0:T(8,128)(2,1)S(1)}, u32[]{:S(2)}, u32[]{:S(2)}) %collective-permute-start.9) | collective-permute-done | bytes 655392 | tf_op jit(solution)/shard_map/ppermute | solution.py:737
  235.0 3.1 collective-permute-done.8
  238.9 1.6 multiply_reduce_fusion
  244.8 1.7 fusion.20
  246.6 1.7 fusion.12
  252.5 4.1 %collective-permute-done.11 = bf16[640,512]{1,0:T(8,128)(2,1)S(1)} collective-permute-done((bf16[640,512]{1,0:T(8,128)(2,1)S(1)}, bf16[640,512]{1,0:T(8,128)(2,1)S(1)}, u32[]{:S(2)}, u32[]{:S(2)}) %collective-permute-start.11) | collective-permute-done | bytes 655392 | tf_op jit(solution)/shard_map/ppermute | solution.py:737
  256.6 2.3 collective-permute-done.10
  259.7 1.6 multiply_reduce_fusion.1
  270.9 2.1 collective-permute-start.13
  286.3 1.7 fusion.141
  287.9 3.6 fusion.136
  294.2 8.1 %convert_element_type.222.low_ref = bf16[12,4,2,2,2,16,512]{6,5,4,3,2,1,0:T(8,128)(2,1)} convert(f32[12,4,2,2,2,16,512]{6,5,4,3,2,1,0:T(8,128)} %constant_dynamic-update-slice_fusion.grads_ref) | non-fusion elementwise | flops 3145728 | bytes 18874368 | tf_op jit(solution)/shard_map/convert_element_type | solution.py:797
  302.4 70.5 %reduce_all.1 = (f32[12,16,512]{2,1,0:T(8,128)}, f32[8,128]{1,0:T(8,128)}) custom-call(f32[12,4,2,2,2,16,512]{6,5,4,3,2,1,0:T(8,128)} %constant_dynamic-update-slice_fusion.grads_ref, bf16[12,4,2,2,2,16,512]{6,5,4,3,2,1,0:T(8,128)(2,1)} %convert_element_type.222.low_ref, f32[8,128]{1,0:T(8,128)} %broadcast_select_fusion.stats_ref), custom_call_target="tpu_custom_call" | custom-call | tf_op jit(solution)/shard_map/reduce_all/pallas_call | solution.py:559
  377.4 2.3 fusion.220
  (335 shorter events, 97.6 us)
Async XLA Ops:
  0.7 7.6 %copy-start.36 = (f32[11,16,512]{2,1,0:T(8,128)S(1)}, f32[11,16,512]{2,1,0:T(8,128)}, u32[]{:S(2)}) copy-start(f32[11,16,512]{2,1,0:T(8,128)} %param.31) | copy-start | bytes 1081348
  0.7 7.6 %copy-start.65 = (f32[16,227]{1,0:T(8,128)S(1)}, f32[16,227]{1,0:T(8,128)}, u32[]{:S(2)}) copy-start(f32[16,227]{1,0:T(8,128)} %param.34) | copy-start | bytes 43588
  0.7 7.7 %copy-start.67 = (f32[227,16]{0,1:T(8,128)S(1)}, f32[227,16]{0,1:T(8,128)}, u32[]{:S(2)}) copy-start(f32[227,16]{0,1:T(8,128)} %param.28) | copy-start | bytes 43588
  0.7 7.7 %copy-start.73 = (f32[4,16]{1,0:T(4,128)S(1)}, f32[4,16]{1,0:T(4,128)}, u32[]{:S(2)}) copy-start(f32[4,16]{1,0:T(4,128)} %param.37) | copy-start | bytes 772
  94.6 4.6 %copy-start.82 = (bf16[640,512]{1,0:T(8,128)(2,1)}, bf16[640,512]{1,0:T(8,128)(2,1)S(1)}, u32[]{:S(2)}) copy-start(bf16[640,512]{1,0:T(8,128)(2,1)S(1)} %fusion.84) | copy-start | bytes 1966084
  99.1 23.3 %copy-start.21 = (bf16[1,4,2,2,2,16,512]{6,5,4,3,2,1,0:T(8,128)(2,1)}, bf16[1,4,2,2,2,16,512]{6,5,4,3,2,1,0:T(8,128)(2,1)S(1)}, u32[]{:S(2)}) copy-start(bf16[1,4,2,2,2,16,512]{6,5,4,3,2,1,0:T(8,128)(2,1)S(1)} %get-tuple-element.87) | copy-start | bytes 1572868
  99.1 24.1 %copy-start.19 = (bf16[1,4,2,2,2,16,512]{6,5,4,3,2,1,0:T(8,128)(2,1)}, bf16[1,4,2,2,2,16,512]{6,5,4,3,2,1,0:T(8,128)(2,1)S(1)}, u32[]{:S(2)}) copy-start(bf16[1,4,2,2,2,16,512]{6,5,4,3,2,1,0:T(8,128)(2,1)S(1)} %get-tuple-element.86) | copy-start | bytes 1572868
  99.1 26.8 %copy-start.23 = (bf16[1,4,2,2,2,16,512]{6,5,4,3,2,1,0:T(8,128)(2,1)}, bf16[1,4,2,2,2,16,512]{6,5,4,3,2,1,0:T(8,128)(2,1)S(1)}, u32[]{:S(2)}) copy-start(bf16[1,4,2,2,2,16,512]{6,5,4,3,2,1,0:T(8,128)(2,1)S(1)} %get-tuple-element.85) | copy-start | bytes 1572868
  99.1 45.3 %copy-start.25 = (bf16[1,4,2,2,2,16,512]{6,5,4,3,2,1,0:T(8,128)(2,1)}, bf16[1,4,2,2,2,16,512]{6,5,4,3,2,1,0:T(8,128)(2,1)S(1)}, u32[]{:S(2)}) copy-start(bf16[1,4,2,2,2,16,512]{6,5,4,3,2,1,0:T(8,128)(2,1)S(1)} %get-tuple-element.84) | copy-start | bytes 1572868
  107.3 15.9 %copy-start.9 = (bf16[1280,512]{1,0:T(8,128)(2,1)}, bf16[1280,512]{1,0:T(8,128)(2,1)S(1)}, u32[]{:S(2)}) copy-start(bf16[1280,512]{1,0:T(8,128)(2,1)S(1)} %multiply_convert_fusion.3) | copy-start | bytes 3932164
  107.3 13.5 %slice-start.2 = ((s8[4915200]{0:T(1024)(128)(4,1)}), s8[4194304]{0:T(1024)(128)(4,1)S(1)}, s32[]{:S(2)}) async-start(s8[4915200]{0:T(1024)(128)(4,1)} %bitcast.277), calls=%async_computation.2 | async-start | bytes 8388608
  107.4 10.1 %collective-permute-start = (bf16[640,512]{1,0:T(8,128)(2,1)S(1)}, bf16[640,512]{1,0:T(8,128)(2,1)S(1)}, u32[]{:S(2)}, u32[]{:S(2)}) collective-permute-start(bf16[640,512]{1,0:T(8,128)(2,1)S(1)} %get-tuple-element.94), channel_id=1, source_target_pairs={{0,1},{1,2},{2,3},{3,6},{6,7},{7,4},{4,5},{5,0},{8,9},{9,10},{10,1... | collective-permute-start | bytes 1966088 | tf_op jit(solution)/shard_map/ppermute | solution.py:720
  107.5 13.3 %collective-permute-start.1 = (bf16[640,512]{1,0:T(8,128)(2,1)S(1)}, bf16[640,512]{1,0:T(8,128)(2,1)S(1)}, u32[]{:S(2)}, u32[]{:S(2)}) collective-permute-start(bf16[640,512]{1,0:T(8,128)(2,1)S(1)} %get-tuple-element.95), channel_id=1, source_target_pairs={{0,5},{1,0},{2,1},{3,2},{6,3},{7,6},{4,7},{5,4},{8,13},{9,8},{10,9... | collective-permute-start | bytes 1966088 | tf_op jit(solution)/shard_map/ppermute | solution.py:721
  131.2 14.1 %copy-start.11 = (bf16[1280,512]{1,0:T(8,128)(2,1)}, bf16[1280,512]{1,0:T(8,128)(2,1)S(1)}, u32[]{:S(2)}) copy-start(bf16[1280,512]{1,0:T(8,128)(2,1)S(1)} %get-tuple-element.69) | copy-start | bytes 3932164
  131.2 10.1 %collective-permute-start.2 = (bf16[640,512]{1,0:T(8,128)(2,1)S(1)}, bf16[640,512]{1,0:T(8,128)(2,1)S(1)}, u32[]{:S(2)}, u32[]{:S(2)}) collective-permute-start(bf16[640,512]{1,0:T(8,128)(2,1)S(1)} %get-tuple-element.92), channel_id=1, source_target_pairs={{0,1},{1,2},{2,3},{3,6},{6,7},{7,4},{4,5},{5,0},{8,9},{9,10},{10,1... | collective-permute-start | bytes 1966088 | tf_op jit(solution)/shard_map/ppermute | solution.py:720
  133.8 9.0 %collective-permute-start.3 = (bf16[640,512]{1,0:T(8,128)(2,1)S(1)}, bf16[640,512]{1,0:T(8,128)(2,1)S(1)}, u32[]{:S(2)}, u32[]{:S(2)}) collective-permute-start(bf16[640,512]{1,0:T(8,128)(2,1)S(1)} %get-tuple-element.93), channel_id=1, source_target_pairs={{0,5},{1,0},{2,1},{3,2},{6,3},{7,6},{4,7},{5,4},{8,13},{9,8},{10,9... | collective-permute-start | bytes 1966088 | tf_op jit(solution)/shard_map/ppermute | solution.py:721
  156.5 12.5 %copy-start.79 = (bf16[2,512,1920]{2,1,0:T(8,128)(2,1)S(1)}, bf16[2,512,1920]{2,1,0:T(8,128)(2,1)}, u32[]{:S(2)}) copy-start(bf16[2,512,1920]{2,1,0:T(8,128)(2,1)} %get-tuple-element.31) | copy-start | bytes 11796484
  159.0 10.1 %collective-permute-start.4 = (bf16[640,512]{1,0:T(8,128)(2,1)S(1)}, bf16[640,512]{1,0:T(8,128)(2,1)S(1)}, u32[]{:S(2)}, u32[]{:S(2)}) collective-permute-start(bf16[640,512]{1,0:T(8,128)(2,1)S(1)} %get-tuple-element.90), channel_id=1, source_target_pairs={{0,1},{1,2},{2,3},{3,6},{6,7},{7,4},{4,5},{5,0},{8,9},{9,10},{10,1... | collective-permute-start | bytes 1966088 | tf_op jit(solution)/shard_map/ppermute | solution.py:720
  162.5 8.5 %collective-permute-start.5 = (bf16[640,512]{1,0:T(8,128)(2,1)S(1)}, bf16[640,512]{1,0:T(8,128)(2,1)S(1)}, u32[]{:S(2)}, u32[]{:S(2)}) collective-permute-start(bf16[640,512]{1,0:T(8,128)(2,1)S(1)} %get-tuple-element.91), channel_id=1, source_target_pairs={{0,5},{1,0},{2,1},{3,2},{6,3},{7,6},{4,7},{5,4},{8,13},{9,8},{10,9... | collective-permute-start | bytes 1966088 | tf_op jit(solution)/shard_map/ppermute | solution.py:721
  198.0 10.4 %copy-start.81 = (bf16[1024,512]{1,0:T(8,128)(2,1)}, bf16[1024,512]{1,0:T(8,128)(2,1)S(1)}, u32[]{:S(2)}) copy-start(bf16[1024,512]{1,0:T(8,128)(2,1)S(1)} %multiply_convert_fusion.4) | copy-start | bytes 3145732
  202.5 5.9 %copy-start.35 = (bf16[2048,512]{1,0:T(8,128)(2,1)S(1)}, bf16[2048,512]{1,0:T(8,128)(2,1)}, u32[]{:S(2)}) copy-start(bf16[2048,512]{1,0:T(8,128)(2,1)} %copy-done.33) | copy-start | bytes 6291460
  202.7 10.4 %collective-permute-start.7 = (bf16[640,512]{1,0:T(8,128)(2,1)S(1)}, bf16[640,512]{1,0:T(8,128)(2,1)S(1)}, u32[]{:S(2)}, u32[]{:S(2)}) collective-permute-start(bf16[640,512]{1,0:T(8,128)(2,1)S(1)} %slice.719), channel_id=1, source_target_pairs={{0,5},{1,0},{2,1},{3,2},{6,3},{7,6},{4,7},{5,4},{8,13},{9,8},{10,9... | collective-permute-start | bytes 1966088 | tf_op jit(solution)/shard_map/ppermute | solution.py:737
  205.0 10.6 %collective-permute-start.6 = (bf16[640,512]{1,0:T(8,128)(2,1)S(1)}, bf16[640,512]{1,0:T(8,128)(2,1)S(1)}, u32[]{:S(2)}, u32[]{:S(2)}) collective-permute-start(bf16[640,512]{1,0:T(8,128)(2,1)S(1)} %slice.720), channel_id=1, source_target_pairs={{0,1},{1,2},{2,3},{3,6},{6,7},{7,4},{4,5},{5,0},{8,9},{9,10},{10,1... | collective-permute-start | bytes 1966088 | tf_op jit(solution)/shard_map/ppermute | solution.py:738
  210.5 5.9 %copy-start.4 = (f32[1280,512]{1,0:T(8,128)S(1)}, f32[1280,512]{1,0:T(8,128)}, u32[]{:S(2)}) copy-start(f32[1280,512]{1,0:T(8,128)} %copy.146) | copy-start | bytes 7864324
  216.4 4.4 %copy-start.88 = (f32[1280,512]{1,0:T(8,128)S(1)}, f32[1280,512]{1,0:T(8,128)}, u32[]{:S(2)}) copy-start(f32[1280,512]{1,0:T(8,128)} %get-tuple-element.123) | copy-start | bytes 7864324
  218.5 4.7 %slice-start.4 = ((s8[4915200]{0:T(1024)(128)(4,1)}), s8[4194304]{0:T(1024)(128)(4,1)S(1)}, s32[]{:S(2)}) async-start(s8[4915200]{0:T(1024)(128)(4,1)} %bitcast.279), calls=%async_computation.4 | async-start | bytes 8388608
  226.8 8.2 %collective-permute-start.9 = (bf16[640,512]{1,0:T(8,128)(2,1)S(1)}, bf16[640,512]{1,0:T(8,128)(2,1)S(1)}, u32[]{:S(2)}, u32[]{:S(2)}) collective-permute-start(bf16[640,512]{1,0:T(8,128)(2,1)S(1)} %slice.717), channel_id=1, source_target_pairs={{0,5},{1,0},{2,1},{3,2},{6,3},{7,6},{4,7},{5,4},{8,13},{9,8},{10,9... | collective-permute-start | bytes 1966088 | tf_op jit(solution)/shard_map/ppermute | solution.py:737
  227.0 11.1 %collective-permute-start.8 = (bf16[640,512]{1,0:T(8,128)(2,1)S(1)}, bf16[640,512]{1,0:T(8,128)(2,1)S(1)}, u32[]{:S(2)}, u32[]{:S(2)}) collective-permute-start(bf16[640,512]{1,0:T(8,128)(2,1)S(1)} %slice.718), channel_id=1, source_target_pairs={{0,1},{1,2},{2,3},{3,6},{6,7},{7,4},{4,5},{5,0},{8,9},{9,10},{10,1... | collective-permute-start | bytes 1966088 | tf_op jit(solution)/shard_map/ppermute | solution.py:738
  230.9 7.9 %copy-start.6 = (f32[1280,512]{1,0:T(8,128)S(1)}, f32[1280,512]{1,0:T(8,128)}, u32[]{:S(2)}) copy-start(f32[1280,512]{1,0:T(8,128)} %copy-done.5) | copy-start | bytes 7864324
  230.9 7.9 %copy-start.58 = (bf16[1,4,2,2,2,16,512]{6,5,4,3,2,1,0:T(8,128)(2,1)S(1)}, bf16[1,4,2,2,2,16,512]{6,5,4,3,2,1,0:T(8,128)(2,1)}, u32[]{:S(2)}) copy-start(bf16[1,4,2,2,2,16,512]{6,5,4,3,2,1,0:T(8,128)(2,1)} %get-tuple-element.83) | copy-start | bytes 1572868
  248.4 8.2 %collective-permute-start.11 = (bf16[640,512]{1,0:T(8,128)(2,1)S(1)}, bf16[640,512]{1,0:T(8,128)(2,1)S(1)}, u32[]{:S(2)}, u32[]{:S(2)}) collective-permute-start(bf16[640,512]{1,0:T(8,128)(2,1)S(1)} %slice.715), channel_id=1, source_target_pairs={{0,5},{1,0},{2,1},{3,2},{6,3},{7,6},{4,7},{5,4},{8,13},{9,8},{10,9... | collective-permute-start | bytes 1966088 | tf_op jit(solution)/shard_map/ppermute | solution.py:737
  248.6 10.3 %collective-permute-start.10 = (bf16[640,512]{1,0:T(8,128)(2,1)S(1)}, bf16[640,512]{1,0:T(8,128)(2,1)S(1)}, u32[]{:S(2)}, u32[]{:S(2)}) collective-permute-start(bf16[640,512]{1,0:T(8,128)(2,1)S(1)} %slice.716), channel_id=1, source_target_pairs={{0,1},{1,2},{2,3},{3,6},{6,7},{7,4},{4,5},{5,0},{8,9},{9,10},{10,1... | collective-permute-start | bytes 1966088 | tf_op jit(solution)/shard_map/ppermute | solution.py:738
  252.5 7.2 %copy-start.2 = (f32[1280,512]{1,0:T(8,128)S(1)}, f32[1280,512]{1,0:T(8,128)}, u32[]{:S(2)}) copy-start(f32[1280,512]{1,0:T(8,128)} %copy-done) | copy-start | bytes 7864324
  252.5 7.2 %copy-start.20 = (bf16[1,4,2,2,2,16,512]{6,5,4,3,2,1,0:T(8,128)(2,1)S(1)}, bf16[1,4,2,2,2,16,512]{6,5,4,3,2,1,0:T(8,128)(2,1)}, u32[]{:S(2)}) copy-start(bf16[1,4,2,2,2,16,512]{6,5,4,3,2,1,0:T(8,128)(2,1)} %copy-done.19) | copy-start | bytes 1572868
  270.7 15.5 %collective-permute-start.12 = (bf16[512,512]{0,1:T(8,128)(2,1)S(1)}, bf16[512,512]{0,1:T(8,128)(2,1)S(1)}, u32[]{:S(2)}, u32[]{:S(2)}) collective-permute-start(bf16[512,512]{0,1:T(8,128)(2,1)S(1)} %slice.722), channel_id=1, source_target_pairs={{0,1},{1,2},{2,3},{3,6},{6,7},{7,4},{4,5},{5,0},{8,9},{9,10},{10,1... | collective-permute-start | bytes 1572872 | tf_op jit(solution)/shard_map/ppermute | solution.py:738
  270.9 15.4 %collective-permute-start.13 = (bf16[512,512]{0,1:T(8,128)(2,1)S(1)}, bf16[512,512]{0,1:T(8,128)(2,1)S(1)}, u32[]{:S(2)}, u32[]{:S(2)}) collective-permute-start(bf16[512,512]{0,1:T(8,128)(2,1)S(1)} %slice.721), channel_id=1, source_target_pairs={{0,5},{1,0},{2,1},{3,2},{6,3},{7,6},{4,7},{5,4},{8,13},{9,8},{10,9... | collective-permute-start | bytes 1572872 | tf_op jit(solution)/shard_map/ppermute | solution.py:737
  302.4 73.6 %copy-start.66 = (f32[16,227]{1,0:T(8,128)S(1)}, f32[16,227]{1,0:T(8,128)}, u32[]{:S(2)}) copy-start(f32[16,227]{1,0:T(8,128)} %param.34) | copy-start | bytes 43588
  302.4 73.6 %copy-start.69 = (f32[16,227]{1,0:T(8,128)S(1)}, f32[16,227]{1,0:T(8,128)}, u32[]{:S(2)}) copy-start(f32[16,227]{1,0:T(8,128)} %param.35) | copy-start | bytes 43588
  302.4 73.6 %copy-start.70 = (f32[16,227]{1,0:T(8,128)S(1)}, f32[16,227]{1,0:T(8,128)}, u32[]{:S(2)}) copy-start(f32[16,227]{1,0:T(8,128)} %param.36) | copy-start | bytes 43588
  302.4 75.0 %copy-start.37 = (f32[11,16,512]{2,1,0:T(8,128)S(1)}, f32[11,16,512]{2,1,0:T(8,128)}, u32[]{:S(2)}) copy-start(f32[11,16,512]{2,1,0:T(8,128)} %param.31) | copy-start | bytes 1081348
  302.4 75.0 %copy-start.63 = (f32[11,16,512]{2,1,0:T(8,128)S(1)}, f32[11,16,512]{2,1,0:T(8,128)}, u32[]{:S(2)}) copy-start(f32[11,16,512]{2,1,0:T(8,128)} %param.32) | copy-start | bytes 1081348
  302.4 75.0 %copy-start.64 = (f32[11,16,512]{2,1,0:T(8,128)S(1)}, f32[11,16,512]{2,1,0:T(8,128)}, u32[]{:S(2)}) copy-start(f32[11,16,512]{2,1,0:T(8,128)} %param.33) | copy-start | bytes 1081348
  373.0 6.7 %copy-start.68 = (f32[227,16]{0,1:T(8,128)S(1)}, f32[227,16]{0,1:T(8,128)}, u32[]{:S(2)}) copy-start(f32[227,16]{0,1:T(8,128)} %param.28) | copy-start | bytes 43588
  373.0 6.7 %copy-start.71 = (f32[227,16]{0,1:T(8,128)S(1)}, f32[227,16]{0,1:T(8,128)}, u32[]{:S(2)}) copy-start(f32[227,16]{0,1:T(8,128)} %param.29) | copy-start | bytes 43588
  373.0 6.7 %copy-start.72 = (f32[227,16]{0,1:T(8,128)S(1)}, f32[227,16]{0,1:T(8,128)}, u32[]{:S(2)}) copy-start(f32[227,16]{0,1:T(8,128)} %param.30) | copy-start | bytes 43588
  373.0 8.1 %copy-start.74 = (f32[4,16]{1,0:T(4,128)S(1)}, f32[4,16]{1,0:T(4,128)}, u32[]{:S(2)}) copy-start(f32[4,16]{1,0:T(4,128)} %param.37) | copy-start | bytes 772
  373.0 8.1 %copy-start.75 = (f32[4,16]{1,0:T(4,128)S(1)}, f32[4,16]{1,0:T(4,128)}, u32[]{:S(2)}) copy-start(f32[4,16]{1,0:T(4,128)} %param.38) | copy-start | bytes 772
  373.0 8.1 %copy-start.76 = (f32[4,16]{1,0:T(4,128)S(1)}, f32[4,16]{1,0:T(4,128)}, u32[]{:S(2)}) copy-start(f32[4,16]{1,0:T(4,128)} %param.39) | copy-start | bytes 772
  (62 other events, 124.4 us)
where the time goes:
time: 390 us; the launch traced here: 383 us
  Pallas kernels  149 us (38%)
  matrix products  79.2 us (20%)
  other arithmetic  52.8 us (14%)
  local copies, waits for them, and re-layouts  41.5 us (11%)
  waiting for transfers between devices  40.1 us (10%)
  starting transfers between devices  16.1 us (4%)
  between operations  4.65 us (1%)
    pallas_call x1, Pallas kernels, gather_all(): pl.pallas_call(functools.partial(gather_kernel, plan, shapes), out_shape=...  78.5 us
    pallas_call x1, Pallas kernels, reduce_all(): pl.pallas_call(functools.partial(reduce_kernel, plan), out_shape=(jax.Sha...  70.5 us
    dot_general x20, matrix products, matmul(): return jnp.dot(a, b, preferred_element_type=jnp.float32)  33.7 us
    unnamed x206, local copies, waits for them, and re-layouts  27.3 us
    dot_general x21, matrix products, left_dot(): lax.dot_general(a, b, (((0,), (0,)), ((), ())), preferred_element_type=jn...  26.7 us
    ppermute x3, waiting for transfers between devices, extended(): before = lax.ppermute(rows[size:], BOTH, plan.ring(1))  20.8 us
    dot_general x12, matrix products, right_dot(): lax.dot_general(a, b, (((1,), (1,)), ((), ())), preferred_element_type=jn...  18.8 us
    ppermute x4, waiting for transfers between devices, collect_back(): from_right = lax.ppermute(before, BOTH, plan.ring(-1)).astype(jnp.float32)  10.6 us
  transfers between devices with their start and end apart: 14, of which 10 were waited for; matrix products, arithmetic and copies ran while one was open for 8% of the time, Pallas kernels for 0%

commit v1 on v0

--- a/solution.py
+++ b/solution.py
@@ -44,18 +44,6 @@
         self.bits = self.chips.bit_length() - 1
         width = math.isqrt(self.chips)
         self.width = width if width * width == self.chips else 0
-
-    def device(self, m, j, c):
-        return (m * self.chips + walk(j % self.chips, self.width)) * 2 + c
-
-    def ring(self, step):
-        pairs = []
-        length = 2 * self.chips
-        for m in range(MICRO):
-            for q in range(length):
-                to = (q + step) % length
-                pairs.append((self.device(m, q // 2, q % 2), self.device(m, to // 2, to % 2)))
-        return pairs
 
 
 MESH = pl.DeviceIdType.MESH
@@ -591,39 +579,407 @@
     )(grads, low, stats)
 
 
-def norm_rows(z, gain):
+def sigmoid(value):
+    return 1.0 / (1.0 + jnp.exp(-value))
+
+
+def centred(z):
     mean = jnp.mean(z, axis=-1, keepdims=True)
-    centred = z - mean
-    spread = jnp.mean(centred * centred, axis=-1, keepdims=True)
-    return centred * lax.rsqrt(spread + EPS_NORM) * gain
-
-
-def update_fwd(index, base, agg, mats, gains):
-    pre = matmul(agg, mats[index])
-    if base is not None:
-        pre = pre + matmul(base, mats[3 + index])
-    active = jax.nn.silu(pre).astype(jnp.bfloat16)
-    inner = matmul(active, mats[7 + index])
-    return (norm_rows(inner, gains[index]), (pre, active, inner))
-
-
-def update_bwd(index, base, agg, mats, gains, kept, grad_out):
-    pre, active, inner = kept
-    _, pull = jax.vjp(norm_rows, inner, gains[index])
-    grad_inner, grad_gain = pull(grad_out)
-    inner_low = grad_inner.astype(jnp.bfloat16)
-    grad_second = left_dot(active, inner_low)
-    grad_active = right_dot(inner_low, mats[7 + index])
-    sigma = jax.nn.sigmoid(pre)
-    pre_low = (grad_active * sigma * (1.0 + pre * (1.0 - sigma))).astype(jnp.bfloat16)
-    grad_first = left_dot(agg, pre_low)
-    grad_agg = right_dot(pre_low, mats[index])
-    grad_self = None
-    grad_base = None
-    if base is not None:
-        grad_self = left_dot(base, pre_low)
-        grad_base = right_dot(pre_low, mats[3 + index])
-    return (grad_base, grad_agg, grad_first, grad_self, grad_second, grad_gain)
+    away = z - mean
+    spread = jnp.mean(away * away, axis=-1, keepdims=True)
+    scale = lax.rsqrt(spread + EPS_NORM)
+    return away * scale, scale
+
+
+def train_kernel(
+    plan,
+    variables,
+    pack_ref,
+    cells_ref,
+    halo_ref,
+    enc_ref,
+    proc_ref,
+    dec_ref,
+    grads_ref,
+    low_ref,
+    stats_ref,
+    wts,
+    cells,
+    halo,
+    enc,
+    proc,
+    dec,
+    grid_low,
+    grid_hid,
+    ext,
+    hid,
+    pre,
+    aggs,
+    grid_agg,
+    out_low,
+    grid_pred,
+    act,
+    d_inner,
+    d_pre,
+    d_agg,
+    parcel,
+    gains,
+    gain_grads,
+    stage,
+    stage_low,
+    load_sem,
+    stage_sem,
+    ex_send,
+    ex_recv,
+):
+    spot = Spot(plan)
+    core = spot.core
+    outer, inner = core, 1 - core
+    lanes = halo.shape[-1]
+    last = wts.shape[0] - 1
+    mesh_rows, width = hid.shape[1:]
+    grid_rows = grid_hid.shape[1]
+    ring = 2 * walk(spot.p, plan.width) + core
+
+    loads = {}
+
+    def load(name, src, dst):
+        loads[name] = pltpu.make_async_copy(src, dst, load_sem.at[len(loads)])
+        loads[name].start()
+
+    load("last", pack_ref.at[last], wts.at[last])
+    load("halo", halo_ref, halo)
+    load("cells", cells_ref, cells)
+    load("enc", enc_ref, enc)
+    for n in (0, 7):
+        load(n, pack_ref.at[n], wts.at[n])
+    load("proc", proc_ref, proc)
+    for n in (1, 4, 8, 2, 5, 9):
+        load(n, pack_ref.at[n], wts.at[n])
+    load("dec", dec_ref, dec)
+    for n in (3, 6, 10):
+        load(n, pack_ref.at[n], wts.at[n])
+
+    def near(blk):
+        q = (ring + 2 * blk - 1 + 2 * plan.chips) % (2 * plan.chips)
+        return spot.in_plane(walk(q // 2, plan.width), q % 2)
+
+    barrier = pltpu.get_barrier_semaphore()
+    for side in range(2):
+        pl.semaphore_signal(barrier, inc=1, device_id=near(side), device_id_type=MESH)
+    pl.semaphore_wait(barrier, 2)
+
+    def exchange(turn, blk, src):
+        dst = ext.at[turn % 3, 3 * (1 - blk)]
+        return remote(src, dst, ex_send.at[turn, blk], ex_recv.at[turn, blk], near(blk))
+
+    def arrived(turn, blk):
+        dst = ext.at[turn % 3, 3 * blk]
+        pltpu.make_async_copy(dst, dst, ex_recv.at[turn, 1 - blk]).wait()
+
+    def sent(turn, blk, src):
+        pltpu.make_async_copy(src, src, ex_send.at[turn, blk]).wait()
+
+    def tiles(rows, body):
+        size = rows // 4
+
+        def one(n, _):
+            body(pl.ds(pl.multiple_of(n * size, 16), size))
+            return 0
+
+        lax.fori_loop(0, rows // size, one, 0)
+
+    for name in ("last", "halo", "cells"):
+        loads[name].wait()
+    group = (lanes + variables) // 128 * 128
+    first_gain = lanes + variables - group
+    gains[...] = wts[last, :, group : group + 128].astype(jnp.float32).T
+
+    def gain(k):
+        return gains[first_gain + k : first_gain + k + 1, :]
+
+    gain_grads[...] = jnp.zeros_like(gain_grads)
+    stats_ref[...] = jnp.zeros_like(stats_ref)
+
+    for b in range(4):
+        if b in (0, 3):
+            rows = halo[b // 3]
+        else:
+            rows = cells[(b - 1) * grid_rows : b * grid_rows, :lanes]
+        hidden = right_dot(rows, wts[last, :, :lanes])
+        if b in (1, 2):
+            grid_hid[b - 1] = hidden
+        grid_low[b] = hidden.astype(jnp.bfloat16)
+
+    def forward(k, low_agg, base):
+        value = matmul(low_agg, wts[k])
+        if base is not None:
+            value = value + matmul(base, wts[3 + k])
+        active = (value * sigmoid(value)).astype(jnp.bfloat16)
+        return value, active, matmul(active, wts[7 + k])
+
+    def mesh_forward(k, blk):
+        def body(rows):
+            base = None if k == 0 else ext[k - 1, 1 + blk, rows]
+            value, _, inside = forward(k, aggs[k, blk, rows], base)
+            pre[k, blk, rows] = value
+            result = centred(inside)[0] * gain(k)
+            if k:
+                result = hid[blk, rows] + result
+            hid[blk, rows] = result
+            ext[k, 1 + blk, rows] = result.astype(jnp.bfloat16)
+
+        tiles(mesh_rows, body)
+        exchange(k, blk, ext.at[k, 1 + blk]).start()
+
+    def collect(graph, blk, turn):
+        size = mesh_rows
+        own = pl.ds(pl.multiple_of(size * (1 - blk), 128), 2 * size)
+        rest = pl.ds(pl.multiple_of(2 * size * blk, 128), size)
+        total = matmul(graph[blk, :, own], ext[turn, 1:3].reshape(2 * size, width))
+        arrived(turn, blk)
+        total = total + matmul(graph[blk, :, rest], ext[turn, 3 * blk])
+        return total.astype(jnp.bfloat16)
+
+    loads["enc"].wait()
+    for blk in (outer, inner):
+        senders = grid_low[pl.ds(blk, 3)].reshape(3 * grid_rows, width)
+        aggs[0, blk] = matmul(enc[blk], senders).astype(jnp.bfloat16)
+        if blk is outer:
+            for n in (0, 7):
+                loads[n].wait()
+        mesh_forward(0, blk)
+    loads["proc"].wait()
+    for k in (1, 2):
+        for n in (k, 3 + k, 7 + k):
+            loads[n].wait()
+        for blk in (outer, inner):
+            aggs[k, blk] = collect(proc, blk, k - 1)
+            mesh_forward(k, blk)
+
+    def backward(k, value, active, inside, grad):
+        along, scale = centred(inside)
+        gain_grads[k : k + 1, :] += jnp.sum(along * grad, axis=0, keepdims=True)
+        grad = grad * gain(k)
+        grad = grad - jnp.mean(grad, axis=-1, keepdims=True)
+        grad = scale * (grad - along * jnp.mean(grad * along, axis=-1, keepdims=True))
+        low = grad.astype(jnp.bfloat16)
+        back = right_dot(low, wts[7 + k])
+        sig = sigmoid(value)
+        pre_low = (back * sig * (1.0 + value * (1.0 - sig))).astype(jnp.bfloat16)
+        from_agg = right_dot(pre_low, wts[k]).astype(jnp.bfloat16)
+        return low, pre_low, from_agg
+
+    def send_back(graph, blk, turn, rows):
+        cols = pl.ds(pl.multiple_of(2 * mesh_rows * blk, 128), mesh_rows)
+        if turn > 3:
+            sent(turn - 1, blk, parcel.at[blk])
+        parcel[blk] = left_dot(graph[blk, :, cols], d_agg[blk, pl.ds(0, rows)]).astype(jnp.bfloat16)
+        exchange(turn, blk, parcel.at[blk]).start()
+
+    def own_back(graph, b, rows):
+        total = None
+        for blk in range(2):
+            region = b - blk + 1
+            cols = pl.ds(pl.multiple_of(region * mesh_rows, 128), mesh_rows)
+            part = left_dot(graph[blk, :, cols], d_agg[blk, pl.ds(0, rows)])
+            total = part if total is None else total + part
+        return total
+
+    stages = []
+
+    def put(mat, value):
+        side = len(stages) % 2
+        if len(stages) >= 2:
+            for copy in stages[-2]:
+                copy.wait()
+        stage[side] = value
+        stage_low[side] = value.astype(jnp.bfloat16)
+        copies = (
+            pltpu.make_async_copy(stage.at[side], grads_ref.at[mat], stage_sem.at[side, 0]),
+            pltpu.make_async_copy(stage_low.at[side], low_ref.at[mat], stage_sem.at[side, 1]),
+        )
+        for copy in copies:
+            copy.start()
+        stages.append(copies)
+
+    def flat(value):
+        return value.reshape(value.shape[0] * value.shape[1], value.shape[2])
+
+    loads["dec"].wait()
+    for n in (3, 6, 10):
+        loads[n].wait()
+    for blk in (outer, inner):
+        grid_agg[blk] = collect(dec, blk, 2)
+
+        def body(rows):
+            base = grid_low[1 + blk, rows]
+            value, active, inside = forward(3, grid_agg[blk, rows], base)
+            out = grid_hid[blk, rows] + centred(inside)[0] * gain(3)
+            low = out.astype(jnp.bfloat16)
+            out_low[blk, rows] = low
+            size = low.shape[0]
+            cell = pl.ds(pl.multiple_of(blk * grid_rows + rows.start, 16), size)
+            lane = lax.broadcasted_iota(jnp.int32, (size, 128), 1)
+            tail = cells[cell, group : group + 128].astype(jnp.float32)
+            piece = (lane >= first_gain) & (lane < first_gain + 3)
+            weight = jnp.sum(jnp.where(piece, tail, 0.0), axis=1, keepdims=True)
+            error = matmul(low, wts[last, :, lanes : 2 * lanes])
+            error = error - cells[cell, lanes : 2 * lanes].astype(jnp.float32)
+            place = lax.broadcasted_iota(jnp.int32, error.shape, 1)
+            error = jnp.where(place < variables, error, 0.0)
+            weighted = weight * error
+            loss = jnp.sum(weighted * error, axis=0, keepdims=True)
+            stats_ref[1:2, :] += sum(loss[:, n : n + 128] for n in range(0, lanes, 128))
+            stats_ref[2:3, :] += jnp.sum(jnp.where(lane == 0, weight, 0.0), axis=0, keepdims=True)
+            pred_low = (2.0 * weighted).astype(jnp.bfloat16)
+            grid_pred[blk, rows] = pred_low
+            grad = right_dot(pred_low, wts[last, :, lanes : 2 * lanes])
+            inner_low, pre_low, from_agg = backward(3, value, active, inside, grad)
+            act[blk, rows] = active
+            d_inner[blk, rows] = inner_low
+            d_pre[blk, rows] = pre_low
+            d_agg[blk, rows] = from_agg
+            grid_hid[blk, rows] = grad + right_dot(pre_low, wts[6])
+
+        tiles(grid_rows, body)
+        send_back(dec, blk, 3, grid_rows)
+    used = pl.ds(0, grid_rows)
+    for b in range(2):
+        hid[b] = own_back(dec, b, grid_rows)
+    put(10, left_dot(flat(act[:, used]), flat(d_inner[:, used])))
+    put(3, left_dot(flat(grid_agg[...]), flat(d_pre[:, used])))
+    put(6, left_dot(flat(grid_low[1:3]), flat(d_pre[:, used])))
+    head_grad = left_dot(flat(out_low[...]), flat(grid_pred[...]))
+
+    def finish(turn, blk, total_ref, add):
+        arrived(turn, blk)
+
+        def body(rows):
+            total = total_ref[blk, rows] + ext[turn % 3, 3 * blk, rows].astype(jnp.float32)
+            total = total.astype(jnp.bfloat16).astype(jnp.float32)
+            hid[blk, rows] = hid[blk, rows] + total if add else total
+
+        tiles(mesh_rows, body)
+
+    def mesh_backward(k, blk):
+        def body(rows):
+            value = pre[k, blk, rows]
+            active = (value * sigmoid(value)).astype(jnp.bfloat16)
+            grad = hid[blk, rows]
+            inner_low, pre_low, from_agg = backward(k, value, active, matmul(active, wts[7 + k]), grad)
+            act[blk, rows] = active
+            d_inner[blk, rows] = inner_low
+            d_pre[blk, rows] = pre_low
+            d_agg[blk, rows] = from_agg
+            if k:
+                hid[blk, rows] = grad + right_dot(pre_low, wts[3 + k])
+
+        tiles(mesh_rows, body)
+
+    turn = 3
+    for k in (2, 1):
+        for blk in (outer, inner):
+            finish(turn, blk, hid if k == 2 else pre.at[2], k < 2)
+            mesh_backward(k, blk)
+            send_back(proc, blk, turn + 1, mesh_rows)
+        turn += 1
+        for b in range(2):
+            pre[k, b] = own_back(proc, b, mesh_rows)
+        put(7 + k, left_dot(flat(act[...]), flat(d_inner[...])))
+        put(k, left_dot(flat(aggs[k]), flat(d_pre[...])))
+        put(3 + k, left_dot(flat(ext[k - 1, 1:3]), flat(d_pre[...])))
+    for blk in (outer, inner):
+        finish(turn, blk, pre.at[1], True)
+        mesh_backward(0, blk)
+    put(7, left_dot(flat(act[...]), flat(d_inner[...])))
+    put(0, left_dot(flat(aggs[0]), flat(d_pre[...])))
+    embed_grad = None
+    for b in range(4):
+        total = None
+        for blk in range(2):
+            region = b - blk
+            if 0 <= region < 3:
+                cols = slice(region * grid_rows, (region + 1) * grid_rows)
+                part = left_dot(enc[blk, :, cols], d_agg[blk])
+                total = part if total is None else total + part
+        low = total.astype(jnp.bfloat16)
+        if b in (1, 2):
+            low = (grid_hid[b - 1] + low.astype(jnp.float32)).astype(jnp.bfloat16)
+            rows = cells[(b - 1) * grid_rows : b * grid_rows, :lanes]
+        else:
+            rows = halo[b // 3]
+        part = left_dot(low, rows)
+        embed_grad = part if embed_grad is None else embed_grad + part
+    gains[...] = jnp.zeros_like(gains)
+    gains[first_gain : first_gain + 4, :] = gain_grads[0:4, :]
+    across = gains[...].T
+    split = group - lanes
+    put(
+        last,
+        jnp.concatenate([embed_grad, head_grad[:, :split], head_grad[:, split:] + across], axis=1),
+    )
+    for copies in stages[-2:]:
+        for copy in copies:
+            copy.wait()
+    for blk in range(2):
+        for n in range(3):
+            sent(n, blk, ext.at[n, 1 + blk])
+        sent(5, blk, parcel.at[blk])
+
+
+def train(plan, variables, pack, cells, halo, encoder, processor, decoder):
+    mats, width = pack.shape[0], pack.shape[2]
+    lanes = halo.shape[-1]
+    mesh_rows, grid_rows = encoder.shape[1], decoder.shape[1]
+    any_space = pl.BlockSpec(memory_space=pl.ANY)
+    dma = pltpu.SemaphoreType.DMA
+    low, full = jnp.bfloat16, jnp.float32
+    mesh_pair, grid_pair = (2, mesh_rows, width), (2, grid_rows, width)
+    return pl.pallas_call(
+        functools.partial(train_kernel, plan, variables),
+        out_shape=(
+            jax.ShapeDtypeStruct(pack.shape, full),
+            jax.ShapeDtypeStruct(pack.shape, low),
+            jax.ShapeDtypeStruct((8, 128), full),
+        ),
+        in_specs=[any_space] * 6,
+        out_specs=(any_space, any_space, pl.BlockSpec(memory_space=pltpu.VMEM)),
+        scratch_shapes=[
+            pltpu.VMEM(pack.shape, low),
+            pltpu.VMEM(cells.shape, low),
+            pltpu.VMEM(halo.shape, low),
+            pltpu.VMEM(encoder.shape, low),
+            pltpu.VMEM(processor.shape, low),
+            pltpu.VMEM(decoder.shape, low),
+            pltpu.VMEM((4,) + grid_pair[1:], low),
+            pltpu.VMEM(grid_pair, full),
+            pltpu.VMEM((3, 4) + mesh_pair[1:], low),
+            pltpu.VMEM(mesh_pair, full),
+            pltpu.VMEM((3,) + mesh_pair, full),
+            pltpu.VMEM((3,) + mesh_pair, low),
+            pltpu.VMEM(grid_pair, low),
+            pltpu.VMEM(grid_pair, low),
+            pltpu.VMEM((2, grid_rows, lanes), low),
+            pltpu.VMEM(mesh_pair, low),
+            pltpu.VMEM(mesh_pair, low),
+            pltpu.VMEM(mesh_pair, low),
+            pltpu.VMEM(mesh_pair, low),
+            pltpu.VMEM(mesh_pair, low),
+            pltpu.VMEM((128, width), full),
+            pltpu.VMEM((8, width), full),
+            pltpu.VMEM((2, width, width), full),
+            pltpu.VMEM((2, width, width), low),
+            dma((mats + 5,)),
+            dma((2, 2)),
+            dma((6, 2)),
+            dma((6, 2)),
+        ],
+        compiler_params=pltpu.CompilerParams(
+            collective_id=2, has_side_effects=True, vmem_limit_bytes=63 << 20
+        ),
+        name="train",
+    )(pack, cells, halo, encoder, processor, decoder)
 
 
 def adamw(param, first, second, grad, scale, rate):
@@ -703,98 +1059,11 @@
     gathered, main, halo, encoder, processor, decoder = gather_all(plan, shapes, pack, cells, codes)
     width = pack.shape[2]
     full = gathered.reshape(-1, width, width)
-    mats = full[:-1]
-    embed = full[-1, :, :lanes]
-    head = full[-1, :, lanes:]
-    gains = full[-1, :, lanes + variables : lanes + variables + 4].T.astype(jnp.float32)
     main = main.reshape(-1, 2 * lanes)
-    inputs = main[:, :lanes]
-    wanted = main[:, lanes:]
-    weight = sum(
-        main[:, lanes + variables + n : lanes + variables + n + 1].astype(jnp.float32) for n in range(3)
-    )
     halo = halo.reshape(2, grid_rows, lanes)
-    inputs_ext = jnp.concatenate([halo[0], inputs, halo[1]])
-    def extended(rows):
-        size = rows.shape[0] // 2
-        before = lax.ppermute(rows[size:], BOTH, plan.ring(1))
-        after = lax.ppermute(rows[:size], BOTH, plan.ring(-1))
-        return jnp.concatenate([before, rows, after])
-
-    def collect(graph, ext):
-        size = ext.shape[0] // 4
-        return jnp.concatenate(
-            [matmul(graph[b], ext[b * size : (b + 3) * size]) for b in range(2)]
-        ).astype(jnp.bfloat16)
-
-    def collect_back(graph, grad_agg):
-        low = grad_agg.astype(jnp.bfloat16)
-        size = low.shape[0] // 2
-        pieces = [left_dot(graph[b], low[b * size : (b + 1) * size]) for b in range(2)]
-        rows = pieces[0].shape[0] // 3
-        before = pieces[0][:rows].astype(jnp.bfloat16)
-        after = pieces[1][2 * rows :].astype(jnp.bfloat16)
-        from_right = lax.ppermute(before, BOTH, plan.ring(-1)).astype(jnp.float32)
-        from_left = lax.ppermute(after, BOTH, plan.ring(1)).astype(jnp.float32)
-        first = from_left + pieces[0][rows : 2 * rows] + pieces[1][:rows]
-        second = pieces[0][2 * rows :] + pieces[1][rows : 2 * rows] + from_right
-        return jnp.concatenate([first, second]).astype(jnp.bfloat16).astype(jnp.float32)
-
-    hidden_ext = right_dot(inputs_ext, embed)
-    grid_hidden = hidden_ext[grid_rows : 3 * grid_rows]
-    low_ext = hidden_ext.astype(jnp.bfloat16)
-    grid_low = low_ext[grid_rows : 3 * grid_rows]
-    aggs = [collect(encoder, low_ext)]
-    nodes, kept_first = update_fwd(0, None, aggs[0], mats, gains)
-    kept = [kept_first]
-    lows = [None]
-    for index in (1, 2):
-        mesh_low = nodes.astype(jnp.bfloat16)
-        lows.append(mesh_low)
-        aggs.append(collect(processor, extended(mesh_low)))
-        branch, kept_now = update_fwd(index, mesh_low, aggs[index], mats, gains)
-        kept.append(kept_now)
-        nodes = nodes + branch
-    aggs.append(collect(decoder, extended(nodes.astype(jnp.bfloat16))))
-    branch, kept_now = update_fwd(3, grid_low, aggs[3], mats, gains)
-    kept.append(kept_now)
-    out_low = (grid_hidden + branch).astype(jnp.bfloat16)
-    error = matmul(out_low, head) - wanted.astype(jnp.float32)
-    error = jnp.where(jnp.arange(lanes) < variables, error, 0.0)
-    loss_local = jnp.sum(weight * error * error)
-    weight_local = jnp.sum(weight)
-    grad_pred = (2.0 * weight * error).astype(jnp.bfloat16)
-    grad_head = left_dot(out_low, grad_pred)
-    grad_grid = right_dot(grad_pred, head)
-    pieces = [None] * 11
-    gain_grads = [None] * 4
-    grad_base, grad_agg, pieces[3], pieces[6], pieces[10], gain_grads[3] = update_bwd(
-        3, grid_low, aggs[3], mats, gains, kept[3], grad_grid
-    )
-    grad_grid = grad_grid + grad_base
-    grad_nodes = collect_back(decoder, grad_agg)
-    for index in (2, 1):
-        (
-            grad_base,
-            grad_agg,
-            pieces[index],
-            pieces[3 + index],
-            pieces[7 + index],
-            gain_grads[index],
-        ) = update_bwd(index, lows[index], aggs[index], mats, gains, kept[index], grad_nodes)
-        grad_nodes = grad_nodes + grad_base + collect_back(processor, grad_agg)
-    _, grad_agg, pieces[0], _, pieces[7], gain_grads[0] = update_bwd(
-        0, None, aggs[0], mats, gains, kept[0], grad_nodes
-    )
-    grad_grid = grad_grid + collect_back(encoder, grad_agg)
-    grad_embed = left_dot(grad_grid.astype(jnp.bfloat16), inputs)
-    gain_part = jnp.pad(jnp.stack(gain_grads).T, ((0, 0), (variables, lanes - variables - 4)))
-    pieces.append(jnp.concatenate([grad_embed, grad_head + gain_part], axis=1))
-    grads = jnp.stack(pieces).reshape(gathered.shape)
-    row = jnp.arange(8)[:, None]
-    stats = jnp.where(row == 1, loss_local, jnp.where(row == 2, weight_local, 0.0))
-    stats = jnp.where(jnp.arange(128)[None, :] == 0, stats, 0.0)
-    share, total = reduce_all(plan, grads, grads.astype(jnp.bfloat16), stats)
+    grads, low, stats = train(plan, variables, full, main, halo, encoder, processor, decoder)
+    grads, low = (value.reshape(gathered.shape) for value in (grads, low))
+    share, total = reduce_all(plan, grads, low, stats)
     square_sum, loss_sum, weight_sum = (jnp.sum(total[n]) for n in range(3))
     shares = (
         share[-1, :, :variables].T,

time: 390 us -> 299 us (0.77)
  Pallas kernels: 149 us -> 268 us
  matrix products: 79.2 us -> 0 us
  waiting for transfers between devices: 40.1 us -> 0 us
  local copies, waits for them, and re-layouts: 41.5 us -> 5.26 us
  other arithmetic: 52.8 us -> 16.6 us
  starting transfers between devices: 16.1 us -> 0 us
    pallas_call x0 -> x1, Pallas kernels: none -> 118 us  [train(): pl.pallas_call(functools.partial(train_kernel, plan, variables), out_shap...]
    dot_general x53 -> x0, matrix products: 79.2 us -> none  [the longest x20 33.7 us: matmul(): return jnp.dot(a, b, preferred_element_type=jnp.float32)]
    ppermute x14 -> x0, waiting for transfers between devices: 40.1 us -> none  [the longest x3 20.8 us: extended(): before = lax.ppermute(rows[size:], BOTH, plan.ring(1))]
    unnamed x206 -> x32, local copies, waits for them, and re-layouts: 27.3 us -> 3.5 us
    convert_element_type x6 -> x0, other arithmetic: 17 us -> none  [the longest x1 8.15 us: on_device(): share, total = reduce_all(plan, grads, grads.astype(jnp.bfloat16), stats)]
    ppermute x14 -> x0, starting transfers between devices: 16.1 us -> none  [the longest x3 6.18 us: extended(): before = lax.ppermute(rows[size:], BOTH, plan.ring(1))]
    reduce_sum x10 -> x0, other arithmetic: 14.1 us -> none  [the longest x4 5.84 us: norm_rows(): centred = z - mean]
    dot_general x3 -> x0, local copies, waits for them, and re-layouts: 8.07 us -> none  [the longest x2 5.15 us: matmul(): return jnp.dot(a, b, preferred_element_type=jnp.float32)]
  transfers between devices with their start and end apart: 14 -> 0, of which waited for: 10 -> 0; matrix products, arithmetic and copies ran while one was open for 8% -> 0% of each run, Pallas kernels for 0% -> 0%
where the time goes in v1:
time: 299 us; the launch traced here: 293 us
  Pallas kernels  268 us (90%)
  other arithmetic  16.6 us (6%)
  local copies, waits for them, and re-layouts  5.26 us (2%)
    pallas_call x1, Pallas kernels, train(): pl.pallas_call(functools.partial(train_kernel, plan, variables), out_shap...  118 us
    pallas_call x1, Pallas kernels, gather_all(): pl.pallas_call(functools.partial(gather_kernel, plan, shapes), out_shape=...  78.5 us
    pallas_call x1, Pallas kernels, reduce_all(): pl.pallas_call(functools.partial(reduce_kernel, plan), out_shape=(jax.Sha...  71.2 us

profile of v1, /device:TPU:0, one launch (start us, length us, event | category | flops | bytes accessed | tf_op | source)
XLA Modules:
  0.0 292.7 jit_solution(10379692975372312608)
XLA Ops:
  0.7 0.0 copy-start.3
  0.7 0.7 convert.23
  1.4 1.4 fusion.30
  2.8 0.1 copy.69
  2.9 0.8 fusion.19
  3.6 0.8 slice_add_fusion.2
  4.5 0.7 fusion.15
  5.1 0.7 convert_bitcast_fusion
  5.8 0.7 convert.22
  6.6 0.1 fusion.12
  6.6 0.8 slice_add_fusion.1
  7.5 0.7 fusion.14
  8.1 0.9 slice_add_fusion
  9.0 0.7 fusion.8
  9.7 1.0 convert.20
  10.7 0.2 copy.71
  11.0 1.3 copy.70
  12.3 0.0 copy-done.3
  12.3 0.3 copy.72
  12.6 0.3 fusion.2.cells_ref
  12.9 78.5 %gather_all.1 = (bf16[12,4,2,2,2,16,512]{6,5,4,3,2,1,0:T(8,128)(2,1)}, bf16[2,2,256,512]{3,2,1,0:T(8,128)(2,1)S(1)}, bf16[2,2,256,256]{3,2,1,0:T(8,128)(2,1)S(1)...) custom-call(bf16[12,16,512]{2,1,0:T(8,128)(2,1)S(1)} %pad_maximum_fusion.pack_ref, ...), custom_call_target="tpu_custom_call" | custom-call | tf_op jit(solution)/shard_map/gather_all/pallas_call | solution.py:323
  91.4 0.0 copy-start
  91.4 1.0 copy-done
  92.4 0.8 copy-done.1
  93.2 118.1 %train.1 = (f32[12,512,512]{2,1,0:T(8,128)}, bf16[12,512,512]{2,1,0:T(8,128)(2,1)}, f32[8,128]{1,0:T(8,128)}) custom-call(bf16[12,512,512]{2,1,0:T(8,128)(2,1)} %bitcast.60, bf16[1024,512]{1,0:T(8,128)(2,1)} %bitcast.56, bf16[2,512,256]{2,1,0:T(8,128)(2,1)} %bitcast.57, bf16[2,640,1536]{2,1,0:T(8,128)(2,1)} %get-tuple-element.33.enc_ref, ...), custom_call_target="tpu_custom_call" | custom-call | tf_op jit(solution)/shard_map/train/pallas_call | solution.py:939
  211.4 0.0 copy-start.12
  211.4 0.0 copy-start.13
  211.4 0.0 copy-start.14
  211.4 0.0 copy-start.6
  211.4 0.0 copy-start.8
  211.4 0.0 copy-start.9
  211.4 0.0 copy-start.7
  211.5 0.0 copy-start.10
  211.5 0.0 copy-start.11
  211.5 0.0 copy-start.2
  211.5 0.0 copy-start.4
  211.5 0.0 copy-start.5
  211.5 71.2 %reduce_all.1 = (f32[12,16,512]{2,1,0:T(8,128)}, f32[8,128]{1,0:T(8,128)}) custom-call(f32[12,4,2,2,2,16,512]{6,5,4,3,2,1,0:T(8,128)} %bitcast.58, bf16[12,4,2,2,2,16,512]{6,5,4,3,2,1,0:T(8,128)(2,1)} %bitcast.59, f32[8,128]{1,0:T(8,128)} %get-tuple-element.38.stats_ref), custom_call_target="tpu_custom_call" | custom-call | tf_op jit(solution)/shard_map/reduce_all/pallas_call | solution.py:547
  282.7 1.4 slice_reduce_fusion
  284.8 0.8 slice_multiply_fusion.3
  285.6 0.1 copy.74
  285.7 0.0 copy-done.12
  285.7 0.0 copy-done.13
  285.7 0.6 fusion.22
  286.3 1.4 fusion.24
  287.7 1.4 fusion.28
  289.0 0.0 copy-done.2
  289.1 2.3 fusion.26
  (14 shorter events, 0.1 us)
Async XLA Ops:
  0.7 11.6 %copy-start.3 = (bf16[4,256,227]{1,0,2:T(4,128)(2,1)S(1)}, bf16[4,256,227]{1,0,2:T(4,128)(2,1)}, u32[]{:S(2)}) copy-start(bf16[4,256,227]{1,0,2:T(4,128)(2,1)} %param.21) | copy-start | bytes 1394692
  91.4 1.0 copy-start
  92.4 0.8 copy-start.1
  211.4 74.3 %copy-start.12 = (f32[4,16]{1,0:T(4,128)S(1)}, f32[4,16]{1,0:T(4,128)}, u32[]{:S(2)}) copy-start(f32[4,16]{1,0:T(4,128)} %param.37) | copy-start | bytes 772
  211.4 74.3 %copy-start.13 = (f32[4,16]{1,0:T(4,128)S(1)}, f32[4,16]{1,0:T(4,128)}, u32[]{:S(2)}) copy-start(f32[4,16]{1,0:T(4,128)} %param.38) | copy-start | bytes 772
  211.4 74.3 %copy-start.14 = (f32[4,16]{1,0:T(4,128)S(1)}, f32[4,16]{1,0:T(4,128)}, u32[]{:S(2)}) copy-start(f32[4,16]{1,0:T(4,128)} %param.39) | copy-start | bytes 772
  211.4 74.9 %copy-start.6 = (f32[16,227]{1,0:T(8,128)S(1)}, f32[16,227]{1,0:T(8,128)}, u32[]{:S(2)}) copy-start(f32[16,227]{1,0:T(8,128)} %param.34) | copy-start | bytes 43588
  211.4 74.9 %copy-start.8 = (f32[16,227]{1,0:T(8,128)S(1)}, f32[16,227]{1,0:T(8,128)}, u32[]{:S(2)}) copy-start(f32[16,227]{1,0:T(8,128)} %param.35) | copy-start | bytes 43588
  211.4 74.9 %copy-start.9 = (f32[16,227]{1,0:T(8,128)S(1)}, f32[16,227]{1,0:T(8,128)}, u32[]{:S(2)}) copy-start(f32[16,227]{1,0:T(8,128)} %param.36) | copy-start | bytes 43588
  211.4 76.2 %copy-start.7 = (f32[227,16]{0,1:T(8,128)S(1)}, f32[227,16]{0,1:T(8,128)}, u32[]{:S(2)}) copy-start(f32[227,16]{0,1:T(8,128)} %param.28) | copy-start | bytes 43588
  211.5 76.2 %copy-start.10 = (f32[227,16]{0,1:T(8,128)S(1)}, f32[227,16]{0,1:T(8,128)}, u32[]{:S(2)}) copy-start(f32[227,16]{0,1:T(8,128)} %param.29) | copy-start | bytes 43588
  211.5 76.2 %copy-start.11 = (f32[227,16]{0,1:T(8,128)S(1)}, f32[227,16]{0,1:T(8,128)}, u32[]{:S(2)}) copy-start(f32[227,16]{0,1:T(8,128)} %param.30) | copy-start | bytes 43588
  211.5 77.6 %copy-start.2 = (f32[11,16,512]{2,1,0:T(8,128)S(1)}, f32[11,16,512]{2,1,0:T(8,128)}, u32[]{:S(2)}) copy-start(f32[11,16,512]{2,1,0:T(8,128)} %param.31) | copy-start | bytes 1081348
  211.5 77.6 %copy-start.4 = (f32[11,16,512]{2,1,0:T(8,128)S(1)}, f32[11,16,512]{2,1,0:T(8,128)}, u32[]{:S(2)}) copy-start(f32[11,16,512]{2,1,0:T(8,128)} %param.32) | copy-start | bytes 1081348
  211.5 77.5 %copy-start.5 = (f32[11,16,512]{2,1,0:T(8,128)S(1)}, f32[11,16,512]{2,1,0:T(8,128)}, u32[]{:S(2)}) copy-start(f32[11,16,512]{2,1,0:T(8,128)} %param.33) | copy-start | bytes 1081348
